TPU v7x, 32 devices: a whole 2x2x4 slice. The times are simulated.
32 devices in a mesh: section: 4 (over z), tm: 4 (over y, x), batch: 2 (over core).
Axes of the slice: x: 2, y: 2, z: 4, core: 2. Of those that a mesh axis runs over, the one named last changes fastest.
Arguments:
- acts: bfloat16 [4, 4, 8, 6, 10240], P('section', 'batch', 'tm'), may hold values from -6 to 6
- cot: bfloat16 [4, 8, 6, 10240], P('batch', 'tm'), may hold values from -6 to 6
- spatial_weight: bfloat16 [4, 9, 64, 64], P('section'), may hold values from -0.25 to 0.25
- temporal_weight: bfloat16 [4, 3, 64, 64], P('section'), may hold values from -0.4375 to 0.4375
Outputs:
- grad_in: bfloat16 [4, 4, 8, 6, 10240], P('section', 'batch', 'tm')
- grad_spatial: float32 [4, 9, 64, 64], P('section')
- grad_temporal: float32 [4, 3, 64, 64], P('section')
All inputs are finite; a program needn't handle non-finite values.
Results may differ from a plain program's by a relative error of at most 0.012.
Values may be sent and summed in bfloat16 or wider, within the bound.
A program may use at most 128 MiB of HBM per device.

v0:
```python
import jax
import jax.numpy as jnp
from jax import lax
from jax.sharding import PartitionSpec as P

TIME_DILATION = 2


def from_behind(value, axis, steps):
    count = lax.axis_size(axis)
    first, last = (max(0, -steps), min(count, count - steps))
    return lax.ppermute(value, axis, [(source, source + steps) for source in range(first, last)])


def split_pixels(a, chans):
    return a.reshape(a.shape[:-1] + (a.shape[-1] // chans, chans))


def paired_kernel(kernel):
    return jnp.kron(jnp.eye(2, dtype=kernel.dtype), kernel)


def spatial_fwd(x, ws):
    rows, width = (x.shape[1], x.shape[2])
    chans = ws.shape[-1]
    padded = jnp.pad(x, ((0, 0), (1, 1), (chans, chans)))
    total = jnp.zeros(x.shape, jnp.float32)
    for i in range(3):
        for j in range(3):
            piece = split_pixels(padded[:, i : i + rows, j * chans : j * chans + width], 2 * chans)
            total = total + jnp.einsum(
                "nrpa,ab->nrpb",
                piece,
                paired_kernel(ws[3 * i + j]),
                preferred_element_type=jnp.float32,
            ).reshape(x.shape)
    return total


def spatial_back(gz, x, ws):
    rows, width = (x.shape[1], x.shape[2])
    chans = ws.shape[-1]
    xpad = jnp.pad(x, ((0, 0), (1, 1), (chans, chans)))
    gradient_padded = jnp.pad(gz, ((0, 0), (1, 1), (chans, chans)))
    gz_pairs = split_pixels(gz, 2 * chans)
    total = jnp.zeros(x.shape, jnp.float32)
    grads = []
    for i in range(3):
        for j in range(3):
            gpiece = split_pixels(
                gradient_padded[:, 2 - i : 2 - i + rows, (2 - j) * chans : (2 - j) * chans + width],
                2 * chans,
            )
            total = total + jnp.einsum(
                "nrpb,ab->nrpa",
                gpiece,
                paired_kernel(ws[3 * i + j]),
                preferred_element_type=jnp.float32,
            ).reshape(x.shape)
            xpiece = split_pixels(xpad[:, i : i + rows, j * chans : j * chans + width], 2 * chans)
            square = jnp.einsum(
                "nrpa,nrpb->ab", xpiece, gz_pairs, preferred_element_type=jnp.float32
            )
            grads.append(square[:chans, :chans] + square[chans:, chans:])
    return (total, jnp.stack(grads))


def temporal_back(h, gradient_piece, gradient_padded, dilation_step, wt):
    count = gradient_piece.shape[0]
    chans = wt.shape[-1]
    kernel_taps = [
        gradient_padded[2 * dilation_step : 2 * dilation_step + count],
        gradient_piece,
        gradient_padded[0:count],
    ]
    h_pix = split_pixels(h, chans)
    gh = jnp.zeros(gradient_piece.shape, jnp.float32)
    tgrads = []
    for k in range(3):
        tap = split_pixels(kernel_taps[k], chans)
        gh = gh + jnp.einsum(
            "trwd,cd->trwc", tap, wt[k], preferred_element_type=jnp.float32
        ).reshape(gradient_piece.shape)
        tgrads.append(jnp.einsum("trwc,trwd->cd", h_pix, tap, preferred_element_type=jnp.float32))
    return (gh.astype(jnp.bfloat16), jnp.stack(tgrads))


def section_backward(x, gradient_piece, ws, wt):
    dilation_step = TIME_DILATION
    z = spatial_fwd(x, ws)
    sig = jax.nn.sigmoid(z)
    h = (z * sig).astype(jnp.bfloat16)
    deriv = sig * (1.0 + z * (1.0 - sig))
    tile_gradient, h_tile = (
        lax.all_to_all(gradient_piece, "tm", split_axis=2, concat_axis=0, tiled=True),
        lax.all_to_all(h, "tm", split_axis=2, concat_axis=0, tiled=True),
    )
    gradient_padded = jnp.pad(tile_gradient, ((dilation_step, dilation_step), (0, 0), (0, 0)))
    gh_tile, tgrads = temporal_back(h_tile, tile_gradient, gradient_padded, dilation_step, wt)
    gh = lax.all_to_all(gh_tile, "tm", split_axis=0, concat_axis=2, tiled=True)
    gz = (gh.astype(jnp.float32) * deriv).astype(jnp.bfloat16)
    back, sgrads = spatial_back(gz, x, ws)
    result = (gradient_piece.astype(jnp.float32) + back).astype(jnp.bfloat16)
    return (result, sgrads, tgrads)


def body(acts, cot, spatial_weight, temporal_weight):
    section_idx = lax.axis_index("section")
    number_sections = lax.axis_size("section")
    micro = acts.shape[1]
    local_acts = acts[0]
    ws = spatial_weight[0]
    wt = temporal_weight[0]
    received = jnp.zeros(cot.shape[1:], jnp.bfloat16)
    grads_in = jnp.zeros(local_acts.shape, jnp.bfloat16)
    acc_spatial = jnp.zeros(ws.shape, jnp.float32)
    acc_temporal = jnp.zeros(wt.shape, jnp.float32)
    total_turns = micro + number_sections - 1
    for turn in range(total_turns):
        which = jnp.int32(turn) - (number_sections - 1 - section_idx)
        valid = jnp.logical_and(which >= 0, which < micro)
        clipped = jnp.clip(which, 0, micro - 1)
        x_now = lax.dynamic_index_in_dim(local_acts, clipped, 0, keepdims=False)
        top_grad = lax.dynamic_index_in_dim(cot, clipped, 0, keepdims=False)
        incoming = jnp.where(section_idx == number_sections - 1, top_grad, received)
        result, sgrads, tgrads = section_backward(x_now, incoming, ws, wt)
        weight = valid.astype(jnp.float32)
        acc_spatial = acc_spatial + weight * sgrads
        acc_temporal = acc_temporal + weight * tgrads
        select = (jnp.arange(micro, dtype=jnp.int32) == which)[:, None, None, None]
        grads_in = jnp.where(select, result[None], grads_in)
        if turn + 1 < total_turns:
            received = from_behind(result, "section", -1)
    sum_spatial, sum_temporal = lax.psum((acc_spatial, acc_temporal), ("tm", "batch"))
    return (grads_in[None], sum_spatial[None], sum_temporal[None])


def solution(mesh):
    in_specs = (
        P("section", "batch", "tm", None, None),
        P("batch", "tm", None, None),
        P("section", None, None, None),
        P("section", None, None, None),
    )
    out_specs = (
        P("section", "batch", "tm", None, None),
        P("section", None, None, None),
        P("section", None, None, None),
    )
    return jax.shard_map(body, mesh=mesh, in_specs=in_specs, out_specs=out_specs, check_vma=False)
```

profile of v0, /device:TPU:24, one launch (start us, length us, event | category | flops | bytes accessed | tf_op | source)
XLA Modules:
  0.0 929.5 jit_solution(14927379624928204376)
XLA Ops:
  126.4 13.6 %reshape.1686 = bf16[10240,2,6]{2,1,0:T(2,128)(2,1)} reshape(bf16[4,2,15360]{2,1,0:T(2,128)(2,1)} %all-to-all-done) | data formatting | bytes 491520
  140.0 10.6 %copy.624 = bf16[2,6,4,2560]{3,0,2,1:T(2,128)(2,1)S(1)} copy(bf16[2,6,4,2560]{1,0,3,2:T(2,128)(2,1)} %bitcast.1160) | data formatting | bytes 491520 | tf_op jit(solution)/shard_map/all_to_all | solution.py:95
  205.2 10.3 %copy.809 = bf16[2,6,10240]{1,0,2:T(2,128)(2,1)} copy(bf16[2,6,10240]{2,0,1:T(2,128)(2,1)} %get-tuple-element.11) | data formatting | bytes 491520 | tf_op jit(solution)/shard_map/convert_element_type | solution.py:92
  257.1 12.6 %reshape.1696 = bf16[10240,2,6]{2,1,0:T(2,128)(2,1)} reshape(bf16[4,2,15360]{2,1,0:T(2,128)(2,1)S(1)} %all-to-all-done.10) | data formatting | bytes 491520
  269.7 12.2 %copy.902 = bf16[2,6,4,2560]{3,2,0,1:T(4,128)(2,1)S(1)} copy(bf16[2,6,4,2560]{1,0,3,2:T(2,128)(2,1)} %bitcast.1162) | data formatting | bytes 491520 | tf_op jit(solution)/shard_map/all_to_all | solution.py:96
  283.3 12.6 %reshape.1688 = bf16[10240,2,6]{2,1,0:T(2,128)(2,1)} reshape(bf16[4,2,15360]{2,1,0:T(2,128)(2,1)S(1)} %all-to-all-done.2) | data formatting | bytes 491520
  296.0 10.2 %copy.652 = bf16[2,6,4,2560]{3,0,2,1:T(2,128)(2,1)S(1)} copy(bf16[2,6,4,2560]{1,0,3,2:T(2,128)(2,1)} %bitcast.1163) | data formatting | bytes 491520 | tf_op jit(solution)/shard_map/all_to_all | solution.py:95
  366.4 10.3 %copy.812 = bf16[2,6,10240]{1,0,2:T(2,128)(2,1)} copy(bf16[2,6,10240]{2,0,1:T(2,128)(2,1)} %get-tuple-element.9) | data formatting | bytes 491520 | tf_op jit(solution)/shard_map/convert_element_type | solution.py:92
  418.4 12.6 %reshape.1698 = bf16[10240,2,6]{2,1,0:T(2,128)(2,1)} reshape(bf16[4,2,15360]{2,1,0:T(2,128)(2,1)S(1)} %all-to-all-done.11) | data formatting | bytes 491520
  431.1 12.2 %copy.903 = bf16[2,6,4,2560]{3,2,0,1:T(4,128)(2,1)S(1)} copy(bf16[2,6,4,2560]{1,0,3,2:T(2,128)(2,1)} %bitcast.1165) | data formatting | bytes 491520 | tf_op jit(solution)/shard_map/all_to_all | solution.py:96
  444.7 12.6 %reshape.1690 = bf16[10240,2,6]{2,1,0:T(2,128)(2,1)} reshape(bf16[4,2,15360]{2,1,0:T(2,128)(2,1)S(1)} %all-to-all-done.4) | data formatting | bytes 491520
  457.3 10.2 %copy.680 = bf16[2,6,4,2560]{3,0,2,1:T(2,128)(2,1)S(1)} copy(bf16[2,6,4,2560]{1,0,3,2:T(2,128)(2,1)} %bitcast.1166) | data formatting | bytes 491520 | tf_op jit(solution)/shard_map/all_to_all | solution.py:95
  577.8 12.6 %reshape.1700 = bf16[10240,2,6]{2,1,0:T(2,128)(2,1)} reshape(bf16[4,2,15360]{2,1,0:T(2,128)(2,1)S(1)} %all-to-all-done.12) | data formatting | bytes 491520
  590.4 12.2 %copy.904 = bf16[2,6,4,2560]{3,2,0,1:T(4,128)(2,1)S(1)} copy(bf16[2,6,4,2560]{1,0,3,2:T(2,128)(2,1)} %bitcast.1168) | data formatting | bytes 491520 | tf_op jit(solution)/shard_map/all_to_all | solution.py:96
  604.0 12.6 %reshape.1692 = bf16[10240,2,6]{2,1,0:T(2,128)(2,1)} reshape(bf16[4,2,15360]{2,1,0:T(2,128)(2,1)S(1)} %all-to-all-done.6) | data formatting | bytes 491520
  616.6 10.2 %copy.708 = bf16[2,6,4,2560]{3,0,2,1:T(2,128)(2,1)S(1)} copy(bf16[2,6,4,2560]{1,0,3,2:T(2,128)(2,1)} %bitcast.1169) | data formatting | bytes 491520 | tf_op jit(solution)/shard_map/all_to_all | solution.py:95
  735.9 12.6 %reshape.1702 = bf16[10240,2,6]{2,1,0:T(2,128)(2,1)} reshape(bf16[4,2,15360]{2,1,0:T(2,128)(2,1)S(1)} %all-to-all-done.13) | data formatting | bytes 491520
  748.5 12.2 %copy.905 = bf16[2,6,4,2560]{3,2,0,1:T(4,128)(2,1)S(1)} copy(bf16[2,6,4,2560]{1,0,3,2:T(2,128)(2,1)} %bitcast.1171) | data formatting | bytes 491520 | tf_op jit(solution)/shard_map/all_to_all | solution.py:96
  762.1 12.6 %reshape.1694 = bf16[10240,2,6]{2,1,0:T(2,128)(2,1)} reshape(bf16[4,2,15360]{2,1,0:T(2,128)(2,1)S(1)} %all-to-all-done.8) | data formatting | bytes 491520
  774.7 10.2 %copy.736 = bf16[2,6,4,2560]{3,0,2,1:T(2,128)(2,1)S(1)} copy(bf16[2,6,4,2560]{1,0,3,2:T(2,128)(2,1)} %bitcast.1172) | data formatting | bytes 491520 | tf_op jit(solution)/shard_map/all_to_all | solution.py:95
  841.1 10.3 %copy.821 = bf16[2,6,10240]{1,0,2:T(2,128)(2,1)} copy(bf16[2,6,10240]{2,0,1:T(2,128)(2,1)} %get-tuple-element.3) | data formatting | bytes 491520 | tf_op jit(solution)/shard_map/convert_element_type | solution.py:92
  870.4 12.6 %reshape.1704 = bf16[10240,2,6]{2,1,0:T(2,128)(2,1)} reshape(bf16[4,2,15360]{2,1,0:T(2,128)(2,1)S(1)} %all-to-all-done.14) | data formatting | bytes 491520
  883.2 12.3 %copy.906 = bf16[2,6,4,2560]{3,2,0,1:T(4,128)(2,1)S(1)} copy(bf16[2,6,4,2560]{1,0,3,2:T(2,128)(2,1)} %bitcast.1174) | data formatting | bytes 491520 | tf_op jit(solution)/shard_map/all_to_all | solution.py:96
  897.0 23.7 %psum.15 = f32[1,3,64,64]{3,2,1,0:T(8,128)} all-reduce(f32[1,3,64,64]{3,2,1,0:T(8,128)S(1)} %fusion.170), channel_id=1, replica_groups=mesh['section'=4,'tm'=4,'batch'=2] {'tm','batch'}, use_global_device_ids=true, to_apply=%region_1.2 | all-reduce | flops 12288 | bytes 98304 | tf_op jit(solution)/shard_map/psum | solution.py:134
  (836 shorter events, 617.3 us)
Async XLA Ops:
  26.5 99.9 %all-to-all-start = ((bf16[4,2,15360]{2,1,0:T(2,128)(2,1)}), bf16[4,2,15360]{2,1,0:T(2,128)(2,1)}, u32[]{:S(2)}, u32[]{:S(2)}) async-start(bf16[4,2,15360]{2,1,0:T(2,128)(2,1)} %reshape.1685), calls=%async_computation | async-start | bytes 491520 | tf_op jit(solution)/shard_map/all_to_all | solution.py:95
  33.8 160.6 %copy-start.16 = (bf16[128,128,1,1]{1,0,2,3:T(8,128)(2,1)}, bf16[128,128,1,1]{1,0,2,3:T(8,128)(2,1)S(1)}, u32[]{:S(2)}) copy-start(bf16[128,128,1,1]{1,0,2,3:T(8,128)(2,1)S(1)} %reshape.1603) | copy-start | bytes 98308
  33.9 160.8 %copy-start.11 = (bf16[128,128,1,1]{1,0,2,3:T(8,128)(2,1)}, bf16[128,128,1,1]{1,0,2,3:T(8,128)(2,1)S(1)}, u32[]{:S(2)}) copy-start(bf16[128,128,1,1]{1,0,2,3:T(8,128)(2,1)S(1)} %reshape.1604) | copy-start | bytes 98308
  34.1 160.9 %copy-start.6 = (bf16[128,128,1,1]{1,0,2,3:T(8,128)(2,1)}, bf16[128,128,1,1]{1,0,2,3:T(8,128)(2,1)S(1)}, u32[]{:S(2)}) copy-start(bf16[128,128,1,1]{1,0,2,3:T(8,128)(2,1)S(1)} %reshape.1605) | copy-start | bytes 98308
  34.2 162.0 %copy-start.1 = (bf16[128,128,1,1]{1,0,2,3:T(8,128)(2,1)}, bf16[128,128,1,1]{1,0,2,3:T(8,128)(2,1)S(1)}, u32[]{:S(2)}) copy-start(bf16[128,128,1,1]{1,0,2,3:T(8,128)(2,1)S(1)} %reshape.1606) | copy-start | bytes 98308
  153.7 9.9 %all-to-all-start.1 = ((bf16[8,6,2560]{2,1,0:T(8,128)(2,1)}), bf16[8,6,2560]{2,1,0:T(8,128)(2,1)S(1)}, u32[]{:S(2)}, u32[]{:S(2)}) async-start(bf16[8,6,2560]{2,1,0:T(8,128)(2,1)} %reshape.1671), calls=%async_computation.1 | async-start | bytes 655360 | tf_op jit(solution)/shard_map/all_to_all | solution.py:100
  202.7 31.0 %collective-permute-start = (bf16[2,6,10240]{2,0,1:T(2,128)(2,1)S(1)}, bf16[2,6,10240]{2,0,1:T(2,128)(2,1)S(1)}, u32[]{:S(2)}, u32[]{:S(2)}) collective-permute-start(bf16[2,6,10240]{2,0,1:T(2,128)(2,1)S(1)} %add_convert_fusion.5), channel_id=1, source_target_pairs={{8,0},{16,8},{24,16},{9,1},{17,9},{25,17},{10,2},{18,10},{26,18},{... | collective-permute-start | bytes 737288 | tf_op jit(solution)/shard_map/ppermute | solution.py:12
  225.4 26.6 %all-to-all-start.10 = ((bf16[4,2,15360]{2,1,0:T(2,128)(2,1)}), bf16[4,2,15360]{2,1,0:T(2,128)(2,1)S(1)}, u32[]{:S(2)}, u32[]{:S(2)}) async-start(bf16[4,2,15360]{2,1,0:T(2,128)(2,1)} %reshape.1695), calls=%async_computation.10 | async-start | bytes 491520 | tf_op jit(solution)/shard_map/all_to_all | solution.py:96
  252.0 31.3 %all-to-all-start.2 = ((bf16[4,2,15360]{2,1,0:T(2,128)(2,1)}), bf16[4,2,15360]{2,1,0:T(2,128)(2,1)S(1)}, u32[]{:S(2)}, u32[]{:S(2)}) async-start(bf16[4,2,15360]{2,1,0:T(2,128)(2,1)} %reshape.1687), calls=%async_computation.2 | async-start | bytes 491520 | tf_op jit(solution)/shard_map/all_to_all | solution.py:95
  314.8 10.0 %all-to-all-start.3 = ((bf16[8,6,2560]{2,1,0:T(8,128)(2,1)}), bf16[8,6,2560]{2,1,0:T(8,128)(2,1)}, u32[]{:S(2)}, u32[]{:S(2)}) async-start(bf16[8,6,2560]{2,1,0:T(8,128)(2,1)} %reshape.1681), calls=%async_computation.3 | async-start | bytes 655360 | tf_op jit(solution)/shard_map/all_to_all | solution.py:100
  364.0 31.2 %collective-permute-start.1 = (bf16[2,6,10240]{2,0,1:T(2,128)(2,1)S(1)}, bf16[2,6,10240]{2,0,1:T(2,128)(2,1)S(1)}, u32[]{:S(2)}, u32[]{:S(2)}) collective-permute-start(bf16[2,6,10240]{2,0,1:T(2,128)(2,1)S(1)} %add_convert_fusion.4), channel_id=1, source_target_pairs={{8,0},{16,8},{24,16},{9,1},{17,9},{25,17},{10,2},{18,10},{26,18},{... | collective-permute-start | bytes 737288 | tf_op jit(solution)/shard_map/ppermute | solution.py:12
  386.6 26.9 %all-to-all-start.11 = ((bf16[4,2,15360]{2,1,0:T(2,128)(2,1)}), bf16[4,2,15360]{2,1,0:T(2,128)(2,1)S(1)}, u32[]{:S(2)}, u32[]{:S(2)}) async-start(bf16[4,2,15360]{2,1,0:T(2,128)(2,1)} %reshape.1697), calls=%async_computation.11 | async-start | bytes 491520 | tf_op jit(solution)/shard_map/all_to_all | solution.py:96
  413.6 31.1 %all-to-all-start.4 = ((bf16[4,2,15360]{2,1,0:T(2,128)(2,1)}), bf16[4,2,15360]{2,1,0:T(2,128)(2,1)S(1)}, u32[]{:S(2)}, u32[]{:S(2)}) async-start(bf16[4,2,15360]{2,1,0:T(2,128)(2,1)} %reshape.1689), calls=%async_computation.4 | async-start | bytes 491520 | tf_op jit(solution)/shard_map/all_to_all | solution.py:95
  476.2 10.0 %all-to-all-start.5 = ((bf16[8,6,2560]{2,1,0:T(8,128)(2,1)}), bf16[8,6,2560]{2,1,0:T(8,128)(2,1)}, u32[]{:S(2)}, u32[]{:S(2)}) async-start(bf16[8,6,2560]{2,1,0:T(8,128)(2,1)} %reshape.1682), calls=%async_computation.5 | async-start | bytes 655360 | tf_op jit(solution)/shard_map/all_to_all | solution.py:100
  523.5 30.9 %collective-permute-start.2 = (bf16[2,6,10240]{2,0,1:T(2,128)(2,1)S(1)}, bf16[2,6,10240]{2,0,1:T(2,128)(2,1)S(1)}, u32[]{:S(2)}, u32[]{:S(2)}) collective-permute-start(bf16[2,6,10240]{2,0,1:T(2,128)(2,1)S(1)} %add_convert_fusion.3), channel_id=1, source_target_pairs={{8,0},{16,8},{24,16},{9,1},{17,9},{25,17},{10,2},{18,10},{26,18},{... | collective-permute-start | bytes 737288 | tf_op jit(solution)/shard_map/ppermute | solution.py:12
  545.9 26.8 %all-to-all-start.12 = ((bf16[4,2,15360]{2,1,0:T(2,128)(2,1)}), bf16[4,2,15360]{2,1,0:T(2,128)(2,1)S(1)}, u32[]{:S(2)}, u32[]{:S(2)}) async-start(bf16[4,2,15360]{2,1,0:T(2,128)(2,1)} %reshape.1699), calls=%async_computation.12 | async-start | bytes 491520 | tf_op jit(solution)/shard_map/all_to_all | solution.py:96
  572.7 31.3 %all-to-all-start.6 = ((bf16[4,2,15360]{2,1,0:T(2,128)(2,1)}), bf16[4,2,15360]{2,1,0:T(2,128)(2,1)S(1)}, u32[]{:S(2)}, u32[]{:S(2)}) async-start(bf16[4,2,15360]{2,1,0:T(2,128)(2,1)} %reshape.1691), calls=%async_computation.6 | async-start | bytes 491520 | tf_op jit(solution)/shard_map/all_to_all | solution.py:95
  635.5 10.2 %all-to-all-start.7 = ((bf16[8,6,2560]{2,1,0:T(8,128)(2,1)}), bf16[8,6,2560]{2,1,0:T(8,128)(2,1)}, u32[]{:S(2)}, u32[]{:S(2)}) async-start(bf16[8,6,2560]{2,1,0:T(8,128)(2,1)} %reshape.1683), calls=%async_computation.7 | async-start | bytes 655360 | tf_op jit(solution)/shard_map/all_to_all | solution.py:100
  685.6 27.1 %collective-permute-start.3 = (bf16[2,6,10240]{2,0,1:T(2,128)(2,1)S(1)}, bf16[2,6,10240]{2,0,1:T(2,128)(2,1)S(1)}, u32[]{:S(2)}, u32[]{:S(2)}) collective-permute-start(bf16[2,6,10240]{2,0,1:T(2,128)(2,1)S(1)} %add_convert_fusion.2), channel_id=1, source_target_pairs={{8,0},{16,8},{24,16},{9,1},{17,9},{25,17},{10,2},{18,10},{26,18},{... | collective-permute-start | bytes 737288 | tf_op jit(solution)/shard_map/ppermute | solution.py:12
  707.7 23.3 %all-to-all-start.13 = ((bf16[4,2,15360]{2,1,0:T(2,128)(2,1)}), bf16[4,2,15360]{2,1,0:T(2,128)(2,1)S(1)}, u32[]{:S(2)}, u32[]{:S(2)}) async-start(bf16[4,2,15360]{2,1,0:T(2,128)(2,1)} %reshape.1701), calls=%async_computation.13 | async-start | bytes 491520 | tf_op jit(solution)/shard_map/all_to_all | solution.py:96
  731.0 31.1 %all-to-all-start.8 = ((bf16[4,2,15360]{2,1,0:T(2,128)(2,1)}), bf16[4,2,15360]{2,1,0:T(2,128)(2,1)S(1)}, u32[]{:S(2)}, u32[]{:S(2)}) async-start(bf16[4,2,15360]{2,1,0:T(2,128)(2,1)} %reshape.1693), calls=%async_computation.8 | async-start | bytes 491520 | tf_op jit(solution)/shard_map/all_to_all | solution.py:95
  788.7 9.9 %all-to-all-start.9 = ((bf16[8,6,2560]{2,1,0:T(8,128)(2,1)}), bf16[8,6,2560]{2,1,0:T(8,128)(2,1)S(1)}, u32[]{:S(2)}, u32[]{:S(2)}) async-start(bf16[8,6,2560]{2,1,0:T(8,128)(2,1)} %reshape.1684), calls=%async_computation.9 | async-start | bytes 655360 | tf_op jit(solution)/shard_map/all_to_all | solution.py:100
  793.0 127.7 %all-reduce.17.cloned.1.call-start = ((), (), s32[]{:S(2)}) async-start(), calls=%async_computation.15 | async-start | bytes 589824 | tf_op jit(solution)/shard_map/psum | solution.py:134
  861.3 9.1 all-to-all-start.14
  (175 other events, 2755.1 us)
Sparse Core Ops, SparseCore 0:
  820.6 53.1 all-reduce.16
where the time goes:
time: 944 us; the launch traced here: 930 us
  local copies, waits for them, and re-layouts  609 us (65%)
  matrix products  137 us (15%)
  starting transfers between devices  70 us (7%)
  other arithmetic  49 us (5%)
  blocking collectives  23.7 us (3%)
  waiting for transfers between devices  23.2 us (2%)
  between operations  17.9 us (2%)
    unnamed x379, local copies, waits for them, and re-layouts  229 us
    reshape x105, local copies, waits for them, and re-layouts, split_pixels(): return a.reshape(a.shape[:-1] + (a.shape[-1] // chans, chans))  112 us
    all_to_all x10, local copies, waits for them, and re-layouts, section_backward(): lax.all_to_all(h, 'tm', split_axis=2, concat_axis=0, tiled=True)  61.8 us
    dot_general x45, matrix products, spatial_back(): jnp.einsum('nrpa,nrpb->ab', xpiece, gz_pairs, preferred_element_type=jnp....  54.5 us
    all_to_all x10, local copies, waits for them, and re-layouts, section_backward(): lax.all_to_all(gradient_piece, 'tm', split_axis=2, concat_axis=0, tiled=T...  52.1 us
    convert_element_type x5, local copies, waits for them, and re-layouts, section_backward(): h = (z * sig).astype(jnp.bfloat16)  51.3 us
    select_n x5, local copies, waits for them, and re-layouts, body(): incoming = jnp.where(section_idx == number_sections - 1, top_grad, received)  40.8 us
    dot_general x45, matrix products, spatial_fwd(): jnp.einsum('nrpa,ab->nrpb', piece, paired_kernel(ws[3 * i + j]), preferre...  28.6 us
  transfers between devices with their start and end apart: 20, of which 6 were waited for; matrix products, arithmetic and copies ran while one was open for 48% of the time, Pallas kernels for 0%

commit v1 on v0

--- a/solution.py
+++ b/solution.py
@@ -4,6 +4,29 @@
 from jax.sharding import PartitionSpec as P
 
 TIME_DILATION = 2
+
+
+def in_blocks(array, dim, count):
+    before, after = (array.shape[:dim], array.shape[dim + 1 :])
+    return jnp.moveaxis(array.reshape(*before, count, -1, *after), dim, 0)
+
+
+def in_order(pieces, dim):
+    pieces = jnp.moveaxis(pieces, 0, dim)
+    shape = pieces.shape
+    return pieces.reshape(*shape[:dim], shape[dim] * shape[dim + 1], *shape[dim + 2 :])
+
+
+def sent_to_each(x, axis, split_dim, concat_dim):
+    length, index = (lax.axis_size(axis), lax.axis_index(axis))
+    blocks = in_blocks(x, split_dim, length)
+    result = blocks
+    for lap in range(1, length):
+        target, source = ((index + lap) % length, (index - lap) % length)
+        sent = lax.dynamic_index_in_dim(blocks, target, 0)
+        theirs = lax.ppermute(sent, axis, [(i, (i + lap) % length) for i in range(length)])
+        result = lax.dynamic_update_slice_in_dim(result, theirs, source, axis=0)
+    return in_order(result, concat_dim)
 
 
 def from_behind(value, axis, steps):
@@ -93,7 +116,7 @@
     deriv = sig * (1.0 + z * (1.0 - sig))
     tile_gradient, h_tile = (
         lax.all_to_all(gradient_piece, "tm", split_axis=2, concat_axis=0, tiled=True),
-        lax.all_to_all(h, "tm", split_axis=2, concat_axis=0, tiled=True),
+        sent_to_each(h, "tm", 2, 0),
     )
     gradient_padded = jnp.pad(tile_gradient, ((dilation_step, dilation_step), (0, 0), (0, 0)))
     gh_tile, tgrads = temporal_back(h_tile, tile_gradient, gradient_padded, dilation_step, wt)

time: 944 us -> 828 us (0.88)
  local copies, waits for them, and re-layouts: 609 us -> 446 us
  matrix products: 137 us -> 164 us
  other arithmetic: 49 us -> 73.6 us
    unnamed x379 -> x271, local copies, waits for them, and re-layouts: 229 us -> 117 us
    all_to_all x10 -> x0, local copies, waits for them, and re-layouts: 61.8 us -> none  [section_backward(): lax.all_to_all(h, 'tm', split_axis=2, concat_axis=0, tiled=True)]
    convert_element_type x5 -> x0, local copies, waits for them, and re-layouts: 51.3 us -> none  [section_backward(): h = (z * sig).astype(jnp.bfloat16)]
    dynamic_update_slice x0 -> x20, local copies, waits for them, and re-layouts: none -> 41.7 us  [sent_to_each(): result = lax.dynamic_update_slice_in_dim(result, theirs, source, axis=0)]
    dot_general x45, matrix products: 54.5 us -> 78.8 us  [spatial_back(): jnp.einsum('nrpa,nrpb->ab', xpiece, gz_pairs, preferred_element_type=jnp....]
    all_to_all x5 -> x0, starting transfers between devices: 18 us -> none  [section_backward(): lax.all_to_all(h, 'tm', split_axis=2, concat_axis=0, tiled=True)]
    unnamed x40, other arithmetic: 24.6 us -> 42.6 us
    ppermute x0 -> x15, starting transfers between devices: none -> 17.9 us  [sent_to_each(): lax.ppermute(sent, axis, [(i, (i + lap) % length) for i in range(length)])]
  transfers between devices with their start and end apart: 20 -> 30, of which waited for: 6 -> 5; matrix products, arithmetic and copies ran while one was open for 48% -> 44% of each run, Pallas kernels for 0% -> 0%
where the time goes in v1:
time: 828 us; the launch traced here: 814 us
  local copies, waits for them, and re-layouts  446 us (54%)
  matrix products  164 us (20%)
  other arithmetic  73.6 us (9%)
  starting transfers between devices  68.6 us (8%)
  blocking collectives  23.8 us (3%)
  waiting for transfers between devices  19.8 us (2%)
  between operations  17.6 us (2%)
    unnamed x271, local copies, waits for them, and re-layouts  117 us
    reshape x100, local copies, waits for them, and re-layouts, split_pixels(): return a.reshape(a.shape[:-1] + (a.shape[-1] // chans, chans))  116 us
    dot_general x45, matrix products, spatial_back(): jnp.einsum('nrpa,nrpb->ab', xpiece, gz_pairs, preferred_element_type=jnp....  78.8 us
    all_to_all x10, local copies, waits for them, and re-layouts, section_backward(): lax.all_to_all(gradient_piece, 'tm', split_axis=2, concat_axis=0, tiled=T...  51.9 us
    unnamed x40, other arithmetic  42.6 us
    dynamic_update_slice x20, local copies, waits for them, and re-layouts, sent_to_each(): result = lax.dynamic_update_slice_in_dim(result, theirs, source, axis=0)  41.7 us
    select_n x5, local copies, waits for them, and re-layouts, body(): incoming = jnp.where(section_idx == number_sections - 1, top_grad, received)  40.9 us
    dot_general x45, matrix products, spatial_fwd(): jnp.einsum('nrpa,ab->nrpb', piece, paired_kernel(ws[3 * i + j]), preferre...  31 us
  transfers between devices with their start and end apart: 30, of which 5 were waited for; matrix products, arithmetic and copies ran while one was open for 44% of the time, Pallas kernels for 0%

profile of v1, /device:TPU:24, one launch (start us, length us, event | category | flops | bytes accessed | tf_op | source)
XLA Modules:
  0.0 813.7 jit_solution(13957715892240514445)
XLA Ops:
  8.3 8.2 %copy.603 = bf16[2,6,10240]{1,0,2:T(2,128)(2,1)} copy(bf16[2,6,10240]{2,0,1:T(2,128)(2,1)S(1)} %fusion.326) | data formatting | bytes 491520 | tf_op jit(solution)/shard_map/jit(_where)/select_n | solution.py:148
  16.5 10.0 %reshape.1825 = bf16[4,2,15360]{2,1,0:T(2,128)(2,1)} reshape(bf16[10240,2,6]{2,1,0:T(2,128)(2,1)} %bitcast.1189) | data formatting | bytes 491520
  26.5 4.6 all-to-all-start
  126.4 13.6 %reshape.1826 = bf16[10240,2,6]{2,1,0:T(2,128)(2,1)} reshape(bf16[4,2,15360]{2,1,0:T(2,128)(2,1)} %all-to-all-done) | data formatting | bytes 491520
  140.1 10.5 %copy.604 = bf16[2,6,4,2560]{3,0,2,1:T(2,128)(2,1)S(1)} copy(bf16[2,6,4,2560]{1,0,3,2:T(2,128)(2,1)} %bitcast.1190) | data formatting | bytes 491520 | tf_op jit(solution)/shard_map/all_to_all | solution.py:118
  158.7 4.6 all-to-all-done.1
  221.1 8.2 %copy.631 = bf16[2,6,10240]{1,0,2:T(2,128)(2,1)} copy(bf16[2,6,10240]{2,0,1:T(2,128)(2,1)S(1)} %broadcast_select_fusion.9) | data formatting | bytes 491520 | tf_op jit(solution)/shard_map/jit(_where)/select_n | solution.py:148
  229.2 9.9 %reshape.1827 = bf16[4,2,15360]{2,1,0:T(2,128)(2,1)} reshape(bf16[10240,2,6]{2,1,0:T(2,128)(2,1)} %bitcast.1195) | data formatting | bytes 491520
  253.3 12.6 %reshape.1828 = bf16[10240,2,6]{2,1,0:T(2,128)(2,1)} reshape(bf16[4,2,15360]{2,1,0:T(2,128)(2,1)S(1)} %all-to-all-done.2) | data formatting | bytes 491520
  265.9 10.2 %copy.632 = bf16[2,6,4,2560]{3,0,2,1:T(2,128)(2,1)S(1)} copy(bf16[2,6,4,2560]{1,0,3,2:T(2,128)(2,1)} %bitcast.1191) | data formatting | bytes 491520 | tf_op jit(solution)/shard_map/all_to_all | solution.py:118
  362.2 8.2 %copy.659 = bf16[2,6,10240]{1,0,2:T(2,128)(2,1)} copy(bf16[2,6,10240]{2,0,1:T(2,128)(2,1)S(1)} %broadcast_select_fusion.8) | data formatting | bytes 491520 | tf_op jit(solution)/shard_map/jit(_where)/select_n | solution.py:148
  370.4 9.9 %reshape.1829 = bf16[4,2,15360]{2,1,0:T(2,128)(2,1)} reshape(bf16[10240,2,6]{2,1,0:T(2,128)(2,1)} %bitcast.1196) | data formatting | bytes 491520
  394.3 12.6 %reshape.1830 = bf16[10240,2,6]{2,1,0:T(2,128)(2,1)} reshape(bf16[4,2,15360]{2,1,0:T(2,128)(2,1)S(1)} %all-to-all-done.4) | data formatting | bytes 491520
  406.9 10.2 %copy.660 = bf16[2,6,4,2560]{3,0,2,1:T(2,128)(2,1)S(1)} copy(bf16[2,6,4,2560]{1,0,3,2:T(2,128)(2,1)} %bitcast.1192) | data formatting | bytes 491520 | tf_op jit(solution)/shard_map/all_to_all | solution.py:118
  425.8 4.6 all-to-all-start.5
  499.6 8.2 %copy.687 = bf16[2,6,10240]{1,0,2:T(2,128)(2,1)} copy(bf16[2,6,10240]{2,0,1:T(2,128)(2,1)S(1)} %broadcast_select_fusion.7) | data formatting | bytes 491520 | tf_op jit(solution)/shard_map/jit(_where)/select_n | solution.py:148
  507.7 9.9 %reshape.1831 = bf16[4,2,15360]{2,1,0:T(2,128)(2,1)} reshape(bf16[10240,2,6]{2,1,0:T(2,128)(2,1)} %bitcast.1197) | data formatting | bytes 491520
  531.8 12.6 %reshape.1832 = bf16[10240,2,6]{2,1,0:T(2,128)(2,1)} reshape(bf16[4,2,15360]{2,1,0:T(2,128)(2,1)S(1)} %all-to-all-done.6) | data formatting | bytes 491520
  544.4 10.2 %copy.688 = bf16[2,6,4,2560]{3,0,2,1:T(2,128)(2,1)S(1)} copy(bf16[2,6,4,2560]{1,0,3,2:T(2,128)(2,1)} %bitcast.1193) | data formatting | bytes 491520 | tf_op jit(solution)/shard_map/all_to_all | solution.py:118
  641.9 8.2 %copy.715 = bf16[2,6,10240]{1,0,2:T(2,128)(2,1)} copy(bf16[2,6,10240]{2,0,1:T(2,128)(2,1)S(1)} %broadcast_select_fusion.6) | data formatting | bytes 491520 | tf_op jit(solution)/shard_map/jit(_where)/select_n | solution.py:148
  650.1 9.9 %reshape.1833 = bf16[4,2,15360]{2,1,0:T(2,128)(2,1)} reshape(bf16[10240,2,6]{2,1,0:T(2,128)(2,1)} %bitcast.1198) | data formatting | bytes 491520
  674.0 12.6 %reshape.1834 = bf16[10240,2,6]{2,1,0:T(2,128)(2,1)} reshape(bf16[4,2,15360]{2,1,0:T(2,128)(2,1)S(1)} %all-to-all-done.8) | data formatting | bytes 491520
  686.7 10.2 %copy.716 = bf16[2,6,4,2560]{3,0,2,1:T(2,128)(2,1)S(1)} copy(bf16[2,6,4,2560]{1,0,3,2:T(2,128)(2,1)} %bitcast.1194) | data formatting | bytes 491520 | tf_op jit(solution)/shard_map/all_to_all | solution.py:118
  781.2 23.8 %psum.15 = f32[1,3,64,64]{3,2,1,0:T(8,128)} all-reduce(f32[1,3,64,64]{3,2,1,0:T(8,128)S(1)} %fusion.175), channel_id=1, replica_groups=mesh['section'=4,'tm'=4,'batch'=2] {'tm','batch'}, use_global_device_ids=true, to_apply=%region_1.2 | all-reduce | flops 12288 | bytes 98304 | tf_op jit(solution)/shard_map/psum | solution.py:157
  (773 shorter events, 552.5 us)
Async XLA Ops:
  26.5 100.0 %all-to-all-start = ((bf16[4,2,15360]{2,1,0:T(2,128)(2,1)}), bf16[4,2,15360]{2,1,0:T(2,128)(2,1)}, u32[]{:S(2)}, u32[]{:S(2)}) async-start(bf16[4,2,15360]{2,1,0:T(2,128)(2,1)} %reshape.1825), calls=%async_computation | async-start | bytes 491520 | tf_op jit(solution)/shard_map/all_to_all | solution.py:118
  205.9 43.2 %collective-permute-start.6 = (bf16[1,2,6,2560]{3,0,2,1:T(2,128)(2,1)}, bf16[1,2,6,2560]{3,0,2,1:T(2,128)(2,1)}, u32[]{:S(2)}, u32[]{:S(2)}) collective-permute-start(bf16[1,2,6,2560]{3,0,2,1:T(2,128)(2,1)} %get-tuple-element.20), channel_id=1, source_target_pairs={{0,6},{2,0},{4,2},{6,4},{1,7},{3,1},{5,3},{7,5},{8,14},{10,8},{12,... | collective-permute-start | bytes 184328 | tf_op jit(solution)/shard_map/ppermute | solution.py:27
  207.3 39.0 %collective-permute-start.5 = (bf16[1,2,6,2560]{3,0,2,1:T(2,128)(2,1)}, bf16[1,2,6,2560]{3,0,2,1:T(2,128)(2,1)}, u32[]{:S(2)}, u32[]{:S(2)}) collective-permute-start(bf16[1,2,6,2560]{3,0,2,1:T(2,128)(2,1)} %get-tuple-element.21), channel_id=1, source_target_pairs={{0,4},{2,6},{4,0},{6,2},{1,5},{3,7},{5,1},{7,3},{8,12},{10,14},{12... | collective-permute-start | bytes 184328 | tf_op jit(solution)/shard_map/ppermute | solution.py:27
  208.8 34.9 %collective-permute-start.4 = (bf16[1,2,6,2560]{3,0,2,1:T(2,128)(2,1)}, bf16[1,2,6,2560]{3,0,2,1:T(2,128)(2,1)}, u32[]{:S(2)}, u32[]{:S(2)}) collective-permute-start(bf16[1,2,6,2560]{3,0,2,1:T(2,128)(2,1)} %get-tuple-element.22), channel_id=1, source_target_pairs={{0,2},{2,4},{4,6},{6,0},{1,3},{3,5},{5,7},{7,1},{8,10},{10,12},{12... | collective-permute-start | bytes 184328 | tf_op jit(solution)/shard_map/ppermute | solution.py:27
  239.1 14.1 %all-to-all-start.2 = ((bf16[4,2,15360]{2,1,0:T(2,128)(2,1)}), bf16[4,2,15360]{2,1,0:T(2,128)(2,1)S(1)}, u32[]{:S(2)}, u32[]{:S(2)}) async-start(bf16[4,2,15360]{2,1,0:T(2,128)(2,1)} %reshape.1827), calls=%async_computation.2 | async-start | bytes 491520 | tf_op jit(solution)/shard_map/all_to_all | solution.py:118
  322.4 67.7 %collective-permute-start.9 = (bf16[1,2,6,2560]{3,0,2,1:T(2,128)(2,1)}, bf16[1,2,6,2560]{3,0,2,1:T(2,128)(2,1)}, u32[]{:S(2)}, u32[]{:S(2)}) collective-permute-start(bf16[1,2,6,2560]{3,0,2,1:T(2,128)(2,1)} %get-tuple-element.17), channel_id=1, source_target_pairs={{0,6},{2,0},{4,2},{6,4},{1,7},{3,1},{5,3},{7,5},{8,14},{10,8},{12,... | collective-permute-start | bytes 184328 | tf_op jit(solution)/shard_map/ppermute | solution.py:27
  323.9 63.5 %collective-permute-start.8 = (bf16[1,2,6,2560]{3,0,2,1:T(2,128)(2,1)}, bf16[1,2,6,2560]{3,0,2,1:T(2,128)(2,1)}, u32[]{:S(2)}, u32[]{:S(2)}) collective-permute-start(bf16[1,2,6,2560]{3,0,2,1:T(2,128)(2,1)} %get-tuple-element.18), channel_id=1, source_target_pairs={{0,4},{2,6},{4,0},{6,2},{1,5},{3,7},{5,1},{7,3},{8,12},{10,14},{12... | collective-permute-start | bytes 184328 | tf_op jit(solution)/shard_map/ppermute | solution.py:27
  325.3 59.3 %collective-permute-start.7 = (bf16[1,2,6,2560]{3,0,2,1:T(2,128)(2,1)}, bf16[1,2,6,2560]{3,0,2,1:T(2,128)(2,1)}, u32[]{:S(2)}, u32[]{:S(2)}) collective-permute-start(bf16[1,2,6,2560]{3,0,2,1:T(2,128)(2,1)} %get-tuple-element.19), channel_id=1, source_target_pairs={{0,2},{2,4},{4,6},{6,0},{1,3},{3,5},{5,7},{7,1},{8,10},{10,12},{12... | collective-permute-start | bytes 184328 | tf_op jit(solution)/shard_map/ppermute | solution.py:27
  351.4 10.5 %collective-permute-start.1 = (bf16[2,6,10240]{2,0,1:T(2,128)(2,1)S(1)}, bf16[2,6,10240]{2,0,1:T(2,128)(2,1)S(1)}, u32[]{:S(2)}, u32[]{:S(2)}) collective-permute-start(bf16[2,6,10240]{2,0,1:T(2,128)(2,1)S(1)} %add_convert_fusion.4), channel_id=1, source_target_pairs={{8,0},{16,8},{24,16},{9,1},{17,9},{25,17},{10,2},{18,10},{26,18},{... | collective-permute-start | bytes 737288 | tf_op jit(solution)/shard_map/ppermute | solution.py:35
  380.3 14.0 %all-to-all-start.4 = ((bf16[4,2,15360]{2,1,0:T(2,128)(2,1)}), bf16[4,2,15360]{2,1,0:T(2,128)(2,1)S(1)}, u32[]{:S(2)}, u32[]{:S(2)}) async-start(bf16[4,2,15360]{2,1,0:T(2,128)(2,1)} %reshape.1829), calls=%async_computation.4 | async-start | bytes 491520 | tf_op jit(solution)/shard_map/all_to_all | solution.py:118
  461.8 65.8 %collective-permute-start.12 = (bf16[1,2,6,2560]{3,0,2,1:T(2,128)(2,1)}, bf16[1,2,6,2560]{3,0,2,1:T(2,128)(2,1)}, u32[]{:S(2)}, u32[]{:S(2)}) collective-permute-start(bf16[1,2,6,2560]{3,0,2,1:T(2,128)(2,1)} %get-tuple-element.14), channel_id=1, source_target_pairs={{0,6},{2,0},{4,2},{6,4},{1,7},{3,1},{5,3},{7,5},{8,14},{10,8},{12,... | collective-permute-start | bytes 184328 | tf_op jit(solution)/shard_map/ppermute | solution.py:27
  463.3 61.6 %collective-permute-start.11 = (bf16[1,2,6,2560]{3,0,2,1:T(2,128)(2,1)}, bf16[1,2,6,2560]{3,0,2,1:T(2,128)(2,1)}, u32[]{:S(2)}, u32[]{:S(2)}) collective-permute-start(bf16[1,2,6,2560]{3,0,2,1:T(2,128)(2,1)} %get-tuple-element.15), channel_id=1, source_target_pairs={{0,4},{2,6},{4,0},{6,2},{1,5},{3,7},{5,1},{7,3},{8,12},{10,14},{12... | collective-permute-start | bytes 184328 | tf_op jit(solution)/shard_map/ppermute | solution.py:27
  464.8 57.5 %collective-permute-start.10 = (bf16[1,2,6,2560]{3,0,2,1:T(2,128)(2,1)}, bf16[1,2,6,2560]{3,0,2,1:T(2,128)(2,1)}, u32[]{:S(2)}, u32[]{:S(2)}) collective-permute-start(bf16[1,2,6,2560]{3,0,2,1:T(2,128)(2,1)} %get-tuple-element.16), channel_id=1, source_target_pairs={{0,2},{2,4},{4,6},{6,0},{1,3},{3,5},{5,7},{7,1},{8,10},{10,12},{12... | collective-permute-start | bytes 184328 | tf_op jit(solution)/shard_map/ppermute | solution.py:27
  488.9 10.3 %collective-permute-start.2 = (bf16[2,6,10240]{2,0,1:T(2,128)(2,1)S(1)}, bf16[2,6,10240]{2,0,1:T(2,128)(2,1)S(1)}, u32[]{:S(2)}, u32[]{:S(2)}) collective-permute-start(bf16[2,6,10240]{2,0,1:T(2,128)(2,1)S(1)} %add_convert_fusion.3), channel_id=1, source_target_pairs={{8,0},{16,8},{24,16},{9,1},{17,9},{25,17},{10,2},{18,10},{26,18},{... | collective-permute-start | bytes 737288 | tf_op jit(solution)/shard_map/ppermute | solution.py:35
  517.6 14.2 %all-to-all-start.6 = ((bf16[4,2,15360]{2,1,0:T(2,128)(2,1)}), bf16[4,2,15360]{2,1,0:T(2,128)(2,1)S(1)}, u32[]{:S(2)}, u32[]{:S(2)}) async-start(bf16[4,2,15360]{2,1,0:T(2,128)(2,1)} %reshape.1831), calls=%async_computation.6 | async-start | bytes 491520 | tf_op jit(solution)/shard_map/all_to_all | solution.py:118
  601.0 68.9 %collective-permute-start.15 = (bf16[1,2,6,2560]{3,0,2,1:T(2,128)(2,1)S(1)}, bf16[1,2,6,2560]{3,0,2,1:T(2,128)(2,1)}, u32[]{:S(2)}, u32[]{:S(2)}) collective-permute-start(bf16[1,2,6,2560]{3,0,2,1:T(2,128)(2,1)S(1)} %get-tuple-element.11), channel_id=1, source_target_pairs={{0,6},{2,0},{4,2},{6,4},{1,7},{3,1},{5,3},{7,5},{8,14},{10,8},{12,... | collective-permute-start | bytes 184328 | tf_op jit(solution)/shard_map/ppermute | solution.py:27
  602.5 64.7 %collective-permute-start.14 = (bf16[1,2,6,2560]{3,0,2,1:T(2,128)(2,1)}, bf16[1,2,6,2560]{3,0,2,1:T(2,128)(2,1)}, u32[]{:S(2)}, u32[]{:S(2)}) collective-permute-start(bf16[1,2,6,2560]{3,0,2,1:T(2,128)(2,1)} %get-tuple-element.12), channel_id=1, source_target_pairs={{0,4},{2,6},{4,0},{6,2},{1,5},{3,7},{5,1},{7,3},{8,12},{10,14},{12... | collective-permute-start | bytes 184328 | tf_op jit(solution)/shard_map/ppermute | solution.py:27
  603.9 60.5 %collective-permute-start.13 = (bf16[1,2,6,2560]{3,0,2,1:T(2,128)(2,1)}, bf16[1,2,6,2560]{3,0,2,1:T(2,128)(2,1)}, u32[]{:S(2)}, u32[]{:S(2)}) collective-permute-start(bf16[1,2,6,2560]{3,0,2,1:T(2,128)(2,1)} %get-tuple-element.13), channel_id=1, source_target_pairs={{0,2},{2,4},{4,6},{6,0},{1,3},{3,5},{5,7},{7,1},{8,10},{10,12},{12... | collective-permute-start | bytes 184328 | tf_op jit(solution)/shard_map/ppermute | solution.py:27
  629.8 11.8 %collective-permute-start.3 = (bf16[2,6,10240]{2,0,1:T(2,128)(2,1)S(1)}, bf16[2,6,10240]{2,0,1:T(2,128)(2,1)S(1)}, u32[]{:S(2)}, u32[]{:S(2)}) collective-permute-start(bf16[2,6,10240]{2,0,1:T(2,128)(2,1)S(1)} %add_convert_fusion.2), channel_id=1, source_target_pairs={{8,0},{16,8},{24,16},{9,1},{17,9},{25,17},{10,2},{18,10},{26,18},{... | collective-permute-start | bytes 737288 | tf_op jit(solution)/shard_map/ppermute | solution.py:35
  660.0 14.0 %all-to-all-start.8 = ((bf16[4,2,15360]{2,1,0:T(2,128)(2,1)}), bf16[4,2,15360]{2,1,0:T(2,128)(2,1)S(1)}, u32[]{:S(2)}, u32[]{:S(2)}) async-start(bf16[4,2,15360]{2,1,0:T(2,128)(2,1)} %reshape.1833), calls=%async_computation.8 | async-start | bytes 491520 | tf_op jit(solution)/shard_map/all_to_all | solution.py:118
  705.0 100.0 %all-reduce.17.cloned.1.call-start = ((), (), s32[]{:S(2)}) async-start(), calls=%async_computation.10 | async-start | bytes 589824 | tf_op jit(solution)/shard_map/psum | solution.py:157
  741.9 34.2 %collective-permute-start.18 = (bf16[1,2,6,2560]{3,0,2,1:T(2,128)(2,1)}, bf16[1,2,6,2560]{3,0,2,1:T(2,128)(2,1)}, u32[]{:S(2)}, u32[]{:S(2)}) collective-permute-start(bf16[1,2,6,2560]{3,0,2,1:T(2,128)(2,1)} %get-tuple-element.8), channel_id=1, source_target_pairs={{0,6},{2,0},{4,2},{6,4},{1,7},{3,1},{5,3},{7,5},{8,14},{10,8},{12,... | collective-permute-start | bytes 184328 | tf_op jit(solution)/shard_map/ppermute | solution.py:27
  743.3 30.0 %collective-permute-start.17 = (bf16[1,2,6,2560]{3,0,2,1:T(2,128)(2,1)}, bf16[1,2,6,2560]{3,0,2,1:T(2,128)(2,1)}, u32[]{:S(2)}, u32[]{:S(2)}) collective-permute-start(bf16[1,2,6,2560]{3,0,2,1:T(2,128)(2,1)} %get-tuple-element.9), channel_id=1, source_target_pairs={{0,4},{2,6},{4,0},{6,2},{1,5},{3,7},{5,1},{7,3},{8,12},{10,14},{12... | collective-permute-start | bytes 184328 | tf_op jit(solution)/shard_map/ppermute | solution.py:27
  744.8 25.8 %collective-permute-start.16 = (bf16[1,2,6,2560]{3,0,2,1:T(2,128)(2,1)}, bf16[1,2,6,2560]{3,0,2,1:T(2,128)(2,1)}, u32[]{:S(2)}, u32[]{:S(2)}) collective-permute-start(bf16[1,2,6,2560]{3,0,2,1:T(2,128)(2,1)} %get-tuple-element.10), channel_id=1, source_target_pairs={{0,2},{2,4},{4,6},{6,0},{1,3},{3,5},{5,7},{7,1},{8,10},{10,12},{12... | collective-permute-start | bytes 184328 | tf_op jit(solution)/shard_map/ppermute | solution.py:27
  (136 other events, 2725.5 us)
Sparse Core Ops, SparseCore 0:
  739.5 53.5 all-reduce.16
